TPU v7x, 32 devices: a whole 2x2x4 slice. The times are simulated.
32 devices in a mesh: dp: 8 (over z, x), mp: 4 (over y, core).
Axes of the slice: x: 2, y: 2, z: 4, core: 2. Of those that a mesh axis runs over, the one named last changes fastest.
Arguments:
- teacher_hidden: bfloat16 [4096, 6144], P('dp', 'mp'), may hold values from -4096 to 4096
- teacher_gain: float32 [6144], P('mp'), may hold values from 0.1 to 1.9
- teacher_bias: float32 [6144], P('mp'), may hold values from -3 to 3
- student_feats: bfloat16 [4096, 1024], P(('dp', 'mp')), may hold values from -4096 to 4096
- student_gain: float32 [1024], replicated, may hold values from 0.1 to 1.9
- student_bias: float32 [1024], replicated, may hold values from -3 to 3
- proj_weight: bfloat16 [1024, 6144], P('dp', 'mp'), may hold values from -1.5 to 1.5
Outputs:
- loss: float32 [], replicated
- grad_proj: float32 [1024, 6144], P(None, 'mp')
- grad_feats: bfloat16 [4096, 1024], P(('dp', 'mp'))
- grad_sgain: float32 [1024], replicated
- grad_sbias: float32 [1024], replicated
All inputs are finite; a program needn't handle non-finite values.
Results may differ from a plain program's by a relative error of at most 0.014.
Values may be sent and summed in bfloat16 or wider, within the bound.
A program may use at most 64 MiB of HBM per device.

v0:
```python
import jax
import jax.numpy as jnp
from jax import lax
from jax.sharding import PartitionSpec as P

DT = 6144


epsilon = 1e-06
loss_scale = 512.0


def per_device(
    teacher_hidden,
    teacher_gain,
    teacher_bias,
    student_feats,
    student_gain,
    student_bias,
    proj_weight,
):
    group_rows = teacher_hidden.shape[0]
    own_rows = student_feats.shape[0]
    hidden_vals = teacher_hidden.astype(jnp.float32)
    row_total = lax.psum(jnp.sum(hidden_vals, axis=1), "mp")
    center = hidden_vals - (row_total / DT)[:, None]
    centred_sum = lax.psum(jnp.sum(center * center, axis=1), "mp")
    variance = centred_sum / DT
    target = center * lax.rsqrt(variance + epsilon)[:, None] * teacher_gain + teacher_bias
    raw_rows = lax.all_gather(student_feats, "mp", axis=0, tiled=True)
    values = raw_rows.astype(jnp.float32)
    centred = values - jnp.mean(values, axis=1, keepdims=True)
    scale = lax.rsqrt(jnp.mean(centred * centred, axis=1, keepdims=True) + epsilon)
    student_hat = centred * scale
    normed = (student_hat * student_gain + student_bias).astype(jnp.bfloat16)
    offset = lax.axis_index("mp") * own_rows
    own_hat = lax.dynamic_slice_in_dim(student_hat, offset, own_rows, 0)
    own_scale = lax.dynamic_slice_in_dim(scale, offset, own_rows, 0)
    columns = lax.all_gather(proj_weight, "dp", axis=0, tiled=True)
    projected = jnp.dot(normed, columns, preferred_element_type=jnp.float32)
    dot_terms, sq_proj, sq_target = lax.psum(
        (
            jnp.sum(projected * target, axis=1),
            jnp.sum(projected * projected, axis=1),
            jnp.sum(target * target, axis=1),
        ),
        "mp",
    )
    norm_proj = jnp.sqrt(sq_proj + epsilon)
    norm_target = jnp.sqrt(sq_target + epsilon)
    cosine = dot_terms / (norm_proj * norm_target)
    coef_proj = loss_scale * dot_terms / (norm_proj**3 * norm_target)
    coef_target = loss_scale / (norm_proj * norm_target)
    grad_out = (coef_proj[:, None] * projected - coef_target[:, None] * target).astype(jnp.bfloat16)
    grad_weight = lax.dot_general(
        normed, grad_out, (((0,), (0,)), ((), ())), preferred_element_type=jnp.float32
    )
    grad_normed = lax.psum_scatter(
        lax.dot_general(
            grad_out, columns, (((1,), (1,)), ((), ())), preferred_element_type=jnp.float32
        ).astype(jnp.bfloat16),
        "mp",
        scatter_dimension=0,
        tiled=True,
    ).astype(jnp.float32)
    scaled = grad_normed * student_gain
    grad_feats = (
        own_scale
        * (
            scaled
            - jnp.mean(scaled, axis=1, keepdims=True)
            - own_hat * jnp.mean(scaled * own_hat, axis=1, keepdims=True)
        )
    ).astype(jnp.bfloat16)
    gain_terms = jnp.sum(grad_normed * own_hat, axis=0)
    bias_terms = jnp.sum(grad_normed, axis=0)
    loss_terms = jnp.sum(1.0 - cosine)
    grad_proj, loss_total = (
        lax.psum(grad_weight.astype(jnp.bfloat16), "dp").astype(jnp.float32),
        lax.psum(loss_terms.astype(jnp.bfloat16), "dp").astype(jnp.float32),
    )
    grad_sgain, grad_sbias = lax.psum((gain_terms, bias_terms), ("dp", "mp"))
    loss = loss_total / (group_rows * lax.axis_size("dp"))
    return (loss, grad_proj, grad_feats, grad_sgain, grad_sbias)


def solution(mesh):
    in_specs = (P("dp", "mp"), P("mp"), P("mp"), P(("dp", "mp"), None), P(), P(), P("dp", "mp"))
    out_specs = (P(), P(None, "mp"), P(("dp", "mp"), None), P(), P())
    return jax.shard_map(
        per_device, mesh=mesh, in_specs=in_specs, out_specs=out_specs, check_vma=False
    )
```

profile of v0, /device:TPU:0, one launch (start us, length us, event | category | flops | bytes accessed | tf_op | source)
XLA Modules:
  0.0 281.5 jit_solution(2132056740143326733)
XLA Ops:
  7.2 0.0 copy-start
  7.2 0.0 copy-start.2
  7.2 0.0 copy-start.6
  7.2 0.0 copy-start.4
  7.2 0.0 copy-start.3
  7.2 0.0 all-gather.3.cloned.1.call-start
  7.3 0.7 all-gather.3.cloned.1.call-update
  8.0 0.0 all-gather.5.cloned.1.call-start
  8.0 0.7 all-gather.5.cloned.1.call-update
  8.7 0.0 reduce-scatter.2.cloned.1.call-start
  8.7 1.7 convert_reduce_fusion
  10.4 8.4 %psum.63 = f32[512]{0:T(512)S(1)} all-reduce(f32[512]{0:T(512)S(1)} %convert_reduce_fusion), channel_id=1, replica_groups=mesh['dp'=8,'mp'=4] {'mp'}, use_global_device_ids=true, to_apply=%region_3.0 | all-reduce | flops 512 | bytes 4096 | tf_op jit(solution)/shard_map/psum | solution.py:25
  18.8 0.0 copy-done
  18.8 0.5 fusion.2
  19.4 6.2 %psum.64 = f32[512]{0:T(512)S(1)} all-reduce(f32[512]{0:T(512)S(1)} %fusion.2), channel_id=1, replica_groups=mesh['dp'=8,'mp'=4] {'mp'}, use_global_device_ids=true, to_apply=%region_5.0 | all-reduce | flops 512 | bytes 4096 | tf_op jit(solution)/shard_map/psum | solution.py:27
  25.5 3.7 %all-gather.3.cloned.1.call-done = bf16[512,1024]{1,0:T(8,128)(2,1)} async-done(((bf16[128,1024]{1,0:T(8,128)(2,1)}), bf16[512,1024]{1,0:T(8,128)(2,1)}) %all-gather.3.cloned.1.call-update) | async-done | bytes 1048592 | tf_op jit(solution)/shard_map/all_gather | solution.py:30
  29.2 1.4 convert_reduce_fusion.1
  30.6 1.6 fusion.14
  32.3 59.6 %all-gather.5.cloned.1.call-done = bf16[1024,1536]{1,0:T(8,128)(2,1)} async-done(((bf16[128,1536]{1,0:T(8,128)(2,1)}), bf16[1024,1536]{1,0:T(8,128)(2,1)}) %all-gather.5.cloned.1.call-update) | async-done | bytes 3145744 | tf_op jit(solution)/shard_map/all_gather | solution.py:39
  91.9 0.0 copy-done.2
  91.9 0.0 copy-done.6
  91.9 0.0 copy-done.4
  91.9 0.0 copy-done.3
  91.9 6.1 %multiply_reduce_fusion = (f32[512]{0:T(512)S(1)}, f32[512]{0:T(512)S(1)}, f32[512]{0:T(512)S(1)}, f32[512,1536]{1,0:T(8,128)}) fusion(f32[1536]{0:T(1024)S(1)} %copy-done.3, f32[1536]{0:T(1024)S(1)} %copy-done.4, f32[512]{0:T(512)S(1)} %add_rsqrt_fusion, f32[512]{0:T(512)S(1)} %broadcast_multiply_fusion, bf16[512,1536]{1,0:T(8,128)(2,1)S(1)} %copy-done, ...), kind=kOutput, calls=%fused_computation.15 | convolution fusion | flops 1622407680 | bytes 8947712 | tf_op jit(solution)/shard_map/dot_general | solution.py:40
  97.9 5.8 %all-reduce.1 = (f32[512]{0:T(512)S(1)}, f32[512]{0:T(512)S(1)}, f32[512]{0:T(512)S(1)}) all-reduce(f32[512]{0:T(512)S(1)} %get-tuple-element.6, f32[512]{0:T(512)S(1)} %get-tuple-element.9, f32[512]{0:T(512)S(1)} %get-tuple-element.5), channel_id=1, replica_groups=mesh['dp'=8,'mp'=4] {'mp'}, use_global_device_ids=true, to_apply=%region_7.0 | all-reduce | flops 1536 | bytes 12288 | tf_op jit(solution)/shard_map/psum | solution.py:41
  103.7 0.6 fusion.25
  104.4 0.0 copy-start.5
  104.4 3.0 %fusion.11 = bf16[512,1536]{1,0:T(8,128)(2,1)S(1)} fusion(bf16[512,1536]{1,0:T(8,128)(2,1)S(1)} %copy-done, f32[512,1536]{1,0:T(8,128)} %get-tuple-element.20, f32[512]{0:T(512)S(1)} %get-tuple-element.19, f32[512]{0:T(512)S(1)} %get-tuple-element.17, f32[1536]{0:T(1024)S(1)} %copy-done.3, f32[1536]{0:T(1024)S(1)} %copy-done.4, f32[512]{0:T(512)S(1)} %add_rsqrt_fusion, ...), kind=kLoop, calls=%fused_computation.14 | loop fusion | flops 7077888 | bytes 6311936 | tf_op jit(solution)/shard_map/convert_element_type | solution.py:54
  107.4 0.0 copy-done.5
  107.4 0.0 copy-start.1
  107.4 2.8 convolution_convert_fusion.1
  110.2 0.0 reduce-scatter.2.cloned.1.call-update
  110.2 0.0 all-reduce.4.cloned.1.call-start
  110.3 0.0 copy-done.1
  110.3 3.7 %convolution_convert_fusion = bf16[1024,1536]{1,0:T(8,128)(2,1)} fusion(bf16[512,1536]{1,0:T(8,128)(2,1)S(1)} %fusion.11, f32[1024]{0:T(1024)S(1)} %copy-done.6, f32[1024]{0:T(1024)S(1)} %copy-done.2, bf16[512,1024]{1,0:T(8,128)(2,1)S(1)} %copy-done.1, f32[512]{0:T(512)S(1)} %add_rsqrt_fusion.1, f32[512]{0:T(512)S(1)} %broadcast_multiply_fusion.1), kind=kOutput, calls=%fused_computation.2 | convolution fusion | flops 1615331328 | bytes 5779456 | tf_op jit(solution)/shard_map/dot_general | solution.py:55
  114.0 0.0 all-reduce.4.cloned.1.call-update
  114.0 0.1 dynamic-slice.3
  114.1 0.3 fusion.12
  114.3 20.8 %psum.68 = bf16[]{:T(256)} all-reduce(bf16[]{:T(256)} %get-tuple-element.18), channel_id=1, replica_groups=mesh['dp'=8,'mp'=4] {'dp'}, use_global_device_ids=true, to_apply=%region_13.0 | all-reduce | flops 1 | bytes 4 | tf_op jit(solution)/shard_map/psum | solution.py:80
  135.8 0.0 reduce-scatter.2.cloned.1.call-done
  135.8 1.2 fusion.22
  137.0 41.0 %all-reduce = (f32[1024]{0:T(1024)}, f32[1024]{0:T(1024)}) all-reduce(f32[1024]{0:T(1024)S(1)} %get-tuple-element.7, f32[1024]{0:T(1024)S(1)} %get-tuple-element.11), channel_id=1, replica_groups=mesh['dp'=8,'mp'=4] {'dp','mp'}, use_global_device_ids=true, to_apply=%region_19.0 | all-reduce | flops 2048 | bytes 16384 | tf_op jit(solution)/shard_map/psum | solution.py:82
  178.0 1.8 fusion.20
  179.8 88.5 %all-reduce.4.cloned.1.call-done = bf16[1024,1536]{1,0:T(8,128)(2,1)} async-done(((bf16[1024,1536]{1,0:T(8,128)(2,1)}), bf16[1024,1536]{1,0:T(8,128)(2,1)}) %all-reduce.4.cloned.1.call-update) | async-done | bytes 3145744 | tf_op jit(solution)/shard_map/psum | solution.py:79
  268.3 5.5 %convert_element_type.40 = f32[1024,1536]{1,0:T(8,128)} convert(bf16[1024,1536]{1,0:T(8,128)(2,1)} %all-reduce.4.cloned.1.call-done) | non-fusion elementwise | flops 1572864 | bytes 9437184 | tf_op jit(solution)/shard_map/convert_element_type | solution.py:79
  (5 shorter events, 0.0 us)
Async XLA Ops:
  7.2 11.6 %copy-start = (bf16[512,1536]{1,0:T(8,128)(2,1)S(1)}, bf16[512,1536]{1,0:T(8,128)(2,1)}, u32[]{:S(2)}) copy-start(bf16[512,1536]{1,0:T(8,128)(2,1)} %param.7) | copy-start | bytes 4718596
  7.2 84.7 %copy-start.2 = (f32[1024]{0:T(1024)S(1)}, f32[1024]{0:T(1024)}, u32[]{:S(2)}) copy-start(f32[1024]{0:T(1024)} %param.11) | copy-start | bytes 12292
  7.2 84.7 %copy-start.6 = (f32[1024]{0:T(1024)S(1)}, f32[1024]{0:T(1024)}, u32[]{:S(2)}) copy-start(f32[1024]{0:T(1024)} %param.12) | copy-start | bytes 12292
  7.2 84.7 %copy-start.4 = (f32[1536]{0:T(1024)S(1)}, f32[1536]{0:T(1024)}, u32[]{:S(2)}) copy-start(f32[1536]{0:T(1024)} %param.8) | copy-start | bytes 18436
  7.2 84.7 %copy-start.3 = (f32[1536]{0:T(1024)S(1)}, f32[1536]{0:T(1024)}, u32[]{:S(2)}) copy-start(f32[1536]{0:T(1024)} %param.9) | copy-start | bytes 18436
  7.2 22.0 %all-gather.3.cloned.1.call-start = ((), (), s32[]{:S(2)}) async-start(), calls=%async_computation.1 | async-start | bytes 1310720 | tf_op jit(solution)/shard_map/all_gather | solution.py:30
  8.0 83.9 %all-gather.5.cloned.1.call-start = ((), (), s32[]{:S(2)}) async-start(), calls=%async_computation.2 | async-start | bytes 3538944 | tf_op jit(solution)/shard_map/all_gather | solution.py:39
  8.7 127.1 %reduce-scatter.2.cloned.1.call-start = ((), (), s32[]{:S(2)}) async-start(), calls=%async_computation.4 | async-start | bytes 1310720 | tf_op jit(solution)/shard_map/reduce_scatter | solution.py:58
  104.4 3.0 %copy-start.5 = (bf16[1024,1536]{1,0:T(8,128)(2,1)S(1)}, bf16[1024,1536]{1,0:T(8,128)(2,1)}, u32[]{:S(2)}) copy-start(bf16[1024,1536]{1,0:T(8,128)(2,1)} %all-gather.5.cloned.1.call-done) | copy-start | bytes 9437188
  107.4 2.9 %copy-start.1 = (bf16[512,1024]{1,0:T(8,128)(2,1)S(1)}, bf16[512,1024]{1,0:T(8,128)(2,1)}, u32[]{:S(2)}) copy-start(bf16[512,1024]{1,0:T(8,128)(2,1)} %all-gather.3.cloned.1.call-done) | copy-start | bytes 3145732
  110.2 158.1 %all-reduce.4.cloned.1.call-start = ((), (), s32[]{:S(2)}) async-start(), calls=%async_computation.3 | async-start | bytes 6291456 | tf_op jit(solution)/shard_map/psum | solution.py:79
Sparse Core Ops, SparseCore 0:
  9.6 19.5 all-gather.2
  31.4 60.4 all-gather.4
  110.3 23.7 reduce-scatter.1
  138.5 129.7 all-reduce.3
where the time goes:
time: 282 us; the launch traced here: 281 us
  waiting for transfers between devices  153 us (54%)
  blocking collectives  82.1 us (29%)
  other arithmetic  17.7 us (6%)
  between operations  15.7 us (6%)
  matrix products  12.5 us (4%)
    psum x1, waiting for transfers between devices, per_device(): lax.psum(grad_weight.astype(jnp.bfloat16), 'dp').astype(jnp.float32)  88.5 us
    all_gather x1, waiting for transfers between devices, per_device(): columns = lax.all_gather(proj_weight, 'dp', axis=0, tiled=True)  59.6 us
    psum x1, blocking collectives, per_device(): grad_sgain, grad_sbias = lax.psum((gain_terms, bias_terms), ('dp', 'mp'))  41 us
    psum x1, blocking collectives, per_device(): lax.psum(loss_terms.astype(jnp.bfloat16), 'dp').astype(jnp.float32)  20.8 us
    psum x1, blocking collectives, per_device(): row_total = lax.psum(jnp.sum(hidden_vals, axis=1), 'mp')  8.37 us
    psum x1, blocking collectives, per_device(): centred_sum = lax.psum(jnp.sum(center * center, axis=1), 'mp')  6.17 us
    dot_general x1, matrix products, per_device(): projected = jnp.dot(normed, columns, preferred_element_type=jnp.float32)  6.05 us
    psum x1, blocking collectives, per_device(): lax.psum((jnp.sum(projected * target, axis=1), jnp.sum(projected * projec...  5.8 us
  transfers between devices with their start and end apart: 4, of which 3 were waited for; matrix products, arithmetic and copies ran while one was open for 4% of the time, Pallas kernels for 0%

commit v1 on v0

v1 whole, which is shorter than its diff:
```python
import functools

import jax
import jax.numpy as jnp
from jax import lax
from jax.experimental import pallas as pl
from jax.experimental.pallas import tpu as pltpu
from jax.sharding import PartitionSpec as P

epsilon = 1e-06
loss_scale = 512.0
CHUNK = 64
f32 = jnp.float32
bf16 = jnp.bfloat16


def column_tile(width, most):
    tile = most
    while width % tile:
        tile -= 128
    return tile


def kernel(
    n_dp, n_mp, dt,
    th, tg, tb, sf, sg, sb, w,
    gp_out, gf_out, red_out,
    wfull, gfull, normed, normed_t, own_hat, own_rs, target, proj, go, coef,
    stat_one, stat_two, pb, own_part, rx, zl, zr, zs, gn_send, gn_recv,
    red_mp, red_x, red_z, red_a, red_b, red_c,
    ag_sems, gg_sems, nm_sems, s1_sems, s2_sems, gn_sems, rm_sems, rz_sems, rx_sems, rs_x, rs_r, rs_l, rs_zl, rs_zr,
):
    length = n_dp // 2
    me = lax.axis_index("dp")
    m = lax.axis_index("mp")
    l = me // 2
    p = me % 2
    q = 1 - p
    x_dev = l * 2 + q
    tokens, cols = th.shape
    own, width = sf.shape
    rb = w.shape[0]

    def rows(j, n):
        return pl.ds(pl.multiple_of(j * n, n), n)

    def remote(src, dst, ssem, rsem, device):
        return pltpu.make_async_remote_copy(
            src_ref=src, dst_ref=dst, send_sem=ssem, recv_sem=rsem,
            device_id=device, device_id_type=pl.DeviceIdType.MESH,
        )

    barrier = pltpu.get_barrier_semaphore()
    for k in range(1, n_mp):
        pl.semaphore_signal(barrier, inc=1, device_id={"mp": (m + k) % n_mp}, device_id_type=pl.DeviceIdType.MESH)
    for k in range(1, length):
        pl.semaphore_signal(
            barrier, inc=1, device_id={"dp": ((l + k) % length) * 2 + p}, device_id_type=pl.DeviceIdType.MESH
        )
    pl.semaphore_signal(barrier, inc=1, device_id={"dp": x_dev}, device_id_type=pl.DeviceIdType.MESH)
    pl.semaphore_wait(barrier, n_mp - 1 + length - 1 + 1)

    class Gather:
        def __init__(self, buf, sems):
            self.buf, self.sems = buf, sems

        def block(self, j):
            return self.buf.at[rows(j, rb)]

        def to_right(self, lp):
            ref = self.block(lp * 2 + p)
            return remote(ref, ref, self.sems.at[0, lp], self.sems.at[3, lp], {"dp": lax.rem(me + 2, n_dp)})

        def to_left(self, lp):
            ref = self.block(lp * 2 + p)
            return remote(ref, ref, self.sems.at[1, lp], self.sems.at[3, lp], {"dp": lax.rem(me - 2 + n_dp, n_dp)})

        def to_pair(self, lp):
            ref = self.block(lp * 2 + p)
            return remote(ref, ref, self.sems.at[2, lp], self.sems.at[4, lp], {"dp": x_dev})

        def from_pair(self, lp):
            ref = self.block(lp * 2 + q)
            return remote(ref, ref, self.sems.at[2, lp], self.sems.at[4, lp], {"dp": x_dev})

        def forward_right(self, lp):
            @pl.when(l + 1 < length)
            def _():
                self.to_right(lp).start()

        def forward_left(self, lp):
            @pl.when(l >= 1)
            def _():
                self.to_left(lp).start()

        def begin(self):
            self.forward_right(l)
            self.forward_left(l)
            self.to_pair(l).start()

        def step(self, s):
            a = l - s - 1
            b = l + s + 1

            @pl.when(a >= 0)
            def _():
                self.to_right(a).wait_recv()
                self.forward_right(a)
                self.to_pair(a).start()

            @pl.when(b < length)
            def _():
                self.to_left(b).wait_recv()
                self.forward_left(b)
                self.to_pair(b).start()

        def finish(self):
            for lp in range(length):
                self.from_pair(lp).wait_recv()

        def drain(self):
            for lp in range(length):
                self.to_pair(lp).wait_send()

                @pl.when(jnp.logical_and(lp <= l, l + 1 < length))
                def _():
                    self.to_right(lp).wait_send()

                @pl.when(jnp.logical_and(lp >= l, l >= 1))
                def _():
                    self.to_left(lp).wait_send()

    def mp_peers(make, act):
        for k in range(1, n_mp):
            act(make((m + k) % n_mp))

    def send_all(src, slots, sems):
        mp_peers(lambda d: remote(src(d), slots.at[m], sems.at[0, d], sems.at[1, m], {"mp": d}), lambda c: c.start())

    def recv_all(src, slots, sems):
        mp_peers(lambda d: remote(src(d), slots.at[d], sems.at[0, d], sems.at[1, d], {"mp": d}), lambda c: c.wait_recv())

    def drain_all(src, slots, sems):
        mp_peers(lambda d: remote(src(d), slots.at[m], sems.at[0, d], sems.at[1, m], {"mp": d}), lambda c: c.wait_send())

    gather_w = Gather(wfull, ag_sems)
    wfull[rows(me, rb)] = w[...]
    gather_w.begin()

    for c in range(own // CHUNK):
        r = pl.ds(c * CHUNK, CHUNK)
        v = sf[r].astype(f32)
        v = v - jnp.mean(v, axis=1, keepdims=True)
        rs = lax.rsqrt(jnp.mean(v * v, axis=1, keepdims=True) + epsilon)
        hat = v * rs
        own_hat[r] = hat
        own_rs[r] = jnp.broadcast_to(rs, (CHUNK, 128))
        normed[m, r] = (hat * sg[...] + sb[...]).astype(bf16)
    nm_src = lambda d: normed.at[m]
    send_all(nm_src, normed, nm_sems)

    lane = lax.broadcasted_iota(jnp.int32, (CHUNK, 128), 1)

    @pl.loop(0, tokens // CHUNK)
    def _(c):
        r = rows(c, CHUNK)
        v = th[r].astype(f32)
        mean = jnp.sum(v, axis=1, keepdims=True) / cols
        v = v - mean
        sq = jnp.sum(v * v, axis=1, keepdims=True)
        coef[r] = jnp.where(lane == 0, mean, jnp.where(lane == 1, sq, 0.0))

    stat_one[m] = coef[...].T[0:8]
    s1_src = lambda d: stat_one.at[m]
    send_all(s1_src, stat_one, s1_sems)
    recv_all(s1_src, stat_one, s1_sems)
    mean = stat_one[0, 0:1]
    for k in range(1, n_mp):
        mean = mean + stat_one[k, 0:1]
    mean = mean / n_mp
    total = jnp.zeros_like(mean)
    for k in range(n_mp):
        gap = stat_one[k, 0:1] - mean
        total = total + (stat_one[k, 1:2] + cols * (gap * gap))
    scale = lax.rsqrt(total / dt + epsilon)
    coef[...] = jnp.concatenate([mean, scale, jnp.zeros((126, tokens), f32)], axis=0).T

    @pl.loop(0, tokens // CHUNK)
    def _(c):
        r = rows(c, CHUNK)
        cf = coef[r]
        t = (th[r].astype(f32) - cf[:, 0:1]) * cf[:, 1:2] * tg[...] + tb[...]
        target[r] = t
        coef[r] = jnp.broadcast_to(jnp.sum(t * t, axis=1, keepdims=True), (CHUNK, 128))

    gather_w.step(0)
    recv_all(nm_src, normed, nm_sems)
    for k in range(n_mp):
        normed_t[:, pl.ds(k * own, own)] = normed[k].T
    for s in range(1, length - 1):
        gather_w.step(s)
    gather_w.finish()

    tile = column_tile(cols, 256)

    @pl.loop(0, cols // tile)
    def _(c):
        ct = rows(c, tile)
        proj[:, ct] = jnp.dot(
            normed[...].reshape(tokens, width), wfull[:, ct], preferred_element_type=f32
        )

    @pl.loop(0, tokens // CHUNK)
    def _(c):
        r = rows(c, CHUNK)
        pv, t = proj[r], target[r]
        inner = jnp.sum(pv * t, axis=1, keepdims=True)
        sq = jnp.sum(pv * pv, axis=1, keepdims=True)
        coef[r] = jnp.where(lane == 0, inner, jnp.where(lane == 1, sq, coef[r]))

    stat_two[m] = coef[...].T[0:8]
    s2_src = lambda d: stat_two.at[m]
    send_all(s2_src, stat_two, s2_sems)
    recv_all(s2_src, stat_two, s2_sems)
    sums = stat_two[0]
    for k in range(1, n_mp):
        sums = sums + stat_two[k]
    inner = sums[0:1]
    norm_proj = jnp.sqrt(sums[1:2] + epsilon)
    norm_target = jnp.sqrt(sums[2:3] + epsilon)
    both = norm_proj * norm_target
    loss_part = jnp.sum(1.0 - inner / both, axis=1, keepdims=True)
    coef_proj = loss_scale * inner / (norm_proj * norm_proj * norm_proj * norm_target)
    coef_target = loss_scale / both
    coef[...] = jnp.concatenate([coef_proj, coef_target, jnp.zeros((126, tokens), f32)], axis=0).T

    @pl.loop(0, tokens // CHUNK)
    def _(c):
        r = rows(c, CHUNK)
        cf = coef[r]
        go[r] = (cf[:, 0:1] * proj[r] - cf[:, 1:2] * target[r]).astype(bf16)

    near = jnp.minimum(l, length - 1 - l)
    alone = length - 1 - 2 * near

    def order(i):
        far = jnp.where(2 * l < length, length - 1 - i, i)
        k = jnp.maximum(i - alone, 0)
        d = near - k // 2
        return jnp.where(i < alone, far, jnp.where(k % 2 == 0, l + d, l - d))

    wide = column_tile(cols, 512)

    def partial(j, c):
        return jnp.dot(normed_t[rows(j, rb)], go[:, pl.ds(c * wide, wide)], preferred_element_type=f32)

    def x_copy(lp):
        return remote(pb.at[lp], rx.at[lp], rs_x.at[0, lp], rs_x.at[1, lp], {"dp": x_dev})

    @pl.loop(0, length)
    def _(i):
        lp = order(i)
        for c in range(cols // wide):
            pb[lp, :, pl.ds(c * wide, wide)] = partial(lp * 2 + q, c).astype(bf16)
        x_copy(lp).start()

    @pl.loop(0, length)
    def _(i):
        lp = order(i)
        for c in range(cols // wide):
            own_part[lp, :, pl.ds(c * wide, wide)] = partial(lp * 2 + p, c)

    band = 256

    @pl.loop(0, width // band)
    def _(c):
        ct = rows(c, band)
        g = lax.dot_general(go[...], wfull[ct], (((1,), (1,)), ((), ())), preferred_element_type=f32)
        for k in range(n_mp):
            gn_send[k, :, ct] = g[k * own:(k + 1) * own].astype(bf16)

    gn_src = lambda d: gn_send.at[d]
    send_all(gn_src, gn_recv, gn_sems)
    gn_recv[m] = gn_send[m]

    gather_g = Gather(gfull, gg_sems)

    def right_copy(lp):
        return remote(zs.at[lp], zl.at[lp], rs_r.at[lp], rs_zl.at[lp], {"dp": lax.rem(me + 2, n_dp)})

    def left_copy(lp):
        return remote(zs.at[lp], zr.at[lp], rs_l.at[lp], rs_zr.at[lp], {"dp": lax.rem(me - 2 + n_dp, n_dp)})

    @pl.loop(0, length)
    def _(i):
        lp = order(i)
        x_copy(lp).wait_recv()

        @pl.when(jnp.logical_and(lp >= l, l > 0))
        def _():
            right_copy(lp).wait_recv()
            own_part[lp] = own_part[lp] + zl[lp].astype(f32)

        @pl.when(jnp.logical_and(lp <= l, l < length - 1))
        def _():
            left_copy(lp).wait_recv()
            own_part[lp] = own_part[lp] + zr[lp].astype(f32)

        zs[lp] = (own_part[lp] + rx[lp].astype(f32)).astype(bf16)

        @pl.when(lp > l)
        def _():
            right_copy(lp).start()

        @pl.when(lp < l)
        def _():
            left_copy(lp).start()

    gfull[rows(me, rb)] = zs[l]
    gather_g.begin()

    recv_all(gn_src, gn_recv, gn_sems)
    gain_sum = jnp.zeros((1, width), f32)
    bias_sum = jnp.zeros((1, width), f32)
    for c in range(own // CHUNK):
        r = pl.ds(c * CHUNK, CHUNK)
        g = gn_recv[0, r].astype(f32)
        for k in range(1, n_mp):
            g = g + gn_recv[k, r].astype(f32)
        hat = own_hat[r]
        gain_sum = gain_sum + jnp.sum(g * hat, axis=0, keepdims=True)
        bias_sum = bias_sum + jnp.sum(g, axis=0, keepdims=True)
        g = g * sg[...]
        g = g - jnp.mean(g, axis=1, keepdims=True) - hat * jnp.mean(g * hat, axis=1, keepdims=True)
        gf_out[r] = (own_rs[r][:, 0:1] * g).astype(bf16)
    red_mp[m] = jnp.concatenate(
        [gain_sum, bias_sum, jnp.broadcast_to(loss_part, (1, width)), jnp.zeros((5, width), f32)], axis=0
    )
    rm_src = lambda d: red_mp.at[m]
    send_all(rm_src, red_mp, rm_sems)
    gather_g.step(0)
    recv_all(rm_src, red_mp, rm_sems)
    acc = red_mp[0]
    for k in range(1, n_mp):
        acc = acc + red_mp[k]
    red_a[...] = acc
    pair = remote(red_a, red_x, rx_sems.at[0], rx_sems.at[1], {"dp": x_dev})
    pair.start()
    if length > 2:
        gather_g.step(1)
    pair.wait_recv()
    red_z[l] = red_a[...] + red_x[...]

    def line_copy(d, slot):
        return remote(red_z.at[l], red_z.at[slot], rz_sems.at[0, d], rz_sems.at[1, slot], {"dp": d * 2 + p})

    for k in range(1, length):
        line_copy((l + k) % length, l).start()
    for s in range(2, length - 1):
        gather_g.step(s)
    for k in range(1, length):
        line_copy((l + k) % length, (l + k) % length).wait_recv()
    acc = red_z[0]
    for k in range(1, length):
        acc = acc + red_z[k]
    red_out[...] = acc

    gather_g.finish()
    gp_out[...] = gfull[...]

    gather_w.drain()
    gather_g.drain()
    drain_all(nm_src, normed, nm_sems)
    drain_all(s1_src, stat_one, s1_sems)
    drain_all(s2_src, stat_two, s2_sems)
    drain_all(gn_src, gn_recv, gn_sems)
    drain_all(rm_src, red_mp, rm_sems)
    pair.wait_send()
    for k in range(1, length):
        line_copy((l + k) % length, l).wait_send()
    for lp in range(length):
        x_copy(lp).wait_send()

        @pl.when(lp > l)
        def _():
            right_copy(lp).wait_send()

        @pl.when(lp < l)
        def _():
            left_copy(lp).wait_send()


def per_device(n_dp, n_mp, dt, th, tg, tb, sf, sg, sb, w):
    tokens, cols = th.shape
    own, width = sf.shape
    rb = w.shape[0]
    length = n_dp // 2
    vmem = pltpu.VMEM
    dma = pltpu.SemaphoreType.DMA
    scratch = [
        vmem((width, cols), bf16),
        vmem((width, cols), bf16),
        vmem((n_mp, own, width), bf16),
        vmem((width, tokens), bf16),
        vmem((own, width), f32),
        vmem((own, 128), f32),
        vmem((tokens, cols), f32),
        vmem((tokens, cols), f32),
        vmem((tokens, cols), bf16),
        vmem((tokens, 128), f32),
        vmem((n_mp, 8, tokens), f32),
        vmem((n_mp, 8, tokens), f32),
        vmem((length, rb, cols), bf16),
        vmem((length, rb, cols), f32),
        vmem((length, rb, cols), bf16),
        vmem((length, rb, cols), bf16),
        vmem((length, rb, cols), bf16),
        vmem((length, rb, cols), bf16),
        vmem((n_mp, own, width), bf16),
        vmem((n_mp, own, width), bf16),
        vmem((n_mp, 8, width), f32),
        vmem((8, width), f32),
        vmem((length, 8, width), f32),
        vmem((8, width), f32),
        vmem((8, width), f32),
        vmem((8, width), f32),
        dma((5, length)), dma((5, length)),
        dma((2, n_mp)), dma((2, n_mp)), dma((2, n_mp)), dma((2, n_mp)), dma((2, n_mp)),
        dma((2, length)), dma((2,)), dma((2, length)),
        dma((length,)), dma((length,)), dma((length,)), dma((length,)),
    ]
    whole = pl.BlockSpec(memory_space=pltpu.VMEM)
    grad_proj, grad_feats, sums = pl.pallas_call(
        functools.partial(kernel, n_dp, n_mp, dt),
        out_shape=(
            jax.ShapeDtypeStruct((width, cols), bf16),
            jax.ShapeDtypeStruct((own, width), bf16),
            jax.ShapeDtypeStruct((8, width), f32),
        ),
        in_specs=[whole] * 7,
        out_specs=(whole, whole, whole),
        scratch_shapes=scratch,
        compiler_params=pltpu.CompilerParams(
            collective_id=0, has_side_effects=True, vmem_limit_bytes=56 * 1024 * 1024
        ),
    )(th, tg.reshape(1, -1), tb.reshape(1, -1), sf, sg.reshape(1, -1), sb.reshape(1, -1), w)
    loss = sums[2, 0] / (n_mp * tokens * n_dp)
    return (loss, grad_proj.astype(f32), grad_feats, sums[0], sums[1])


def solution(mesh):
    n_dp, n_mp = mesh.shape["dp"], mesh.shape["mp"]

    def run(th, tg, tb, sf, sg, sb, w):
        in_specs = (P("dp", "mp"), P("mp"), P("mp"), P(("dp", "mp"), None), P(), P(), P("dp", "mp"))
        out_specs = (P(), P(None, "mp"), P(("dp", "mp"), None), P(), P())
        return jax.shard_map(
            functools.partial(per_device, n_dp, n_mp, th.shape[1]),
            mesh=mesh, in_specs=in_specs, out_specs=out_specs, check_vma=False,
        )(th, tg, tb, sf, sg, sb, w)

    return run
```

time: 282 us -> 150 us (0.53)
  waiting for transfers between devices: 153 us -> 0 us
  Pallas kernels: 0 us -> 136 us
  blocking collectives: 82.1 us -> 0 us
  between operations: 15.7 us -> 2.43 us
  matrix products: 12.5 us -> 0 us
  other arithmetic: 17.7 us -> 5.51 us
  local copies, waits for them, and re-layouts: 0.11 us -> 5.93 us
    pallas_call x0 -> x1, Pallas kernels: none -> 136 us  [per_device(): pl.pallas_call(functools.partial(kernel, n_dp, n_mp, dt), out_shape=(jax....]
    psum x1 -> x0, waiting for transfers between devices: 88.5 us -> none  [per_device(): lax.psum(grad_weight.astype(jnp.bfloat16), 'dp').astype(jnp.float32)]
    psum x5 -> x0, blocking collectives: 82.1 us -> none  [the longest x1 41 us: per_device(): grad_sgain, grad_sbias = lax.psum((gain_terms, bias_terms), ('dp', 'mp'))]
    all_gather x2 -> x0, waiting for transfers between devices: 63.2 us -> none  [the longest x1 59.6 us: per_device(): columns = lax.all_gather(proj_weight, 'dp', axis=0, tiled=True)]
    dot_general x3 -> x0, matrix products: 12.5 us -> none  [the longest x1 6.05 us: per_device(): projected = jnp.dot(normed, columns, preferred_element_type=jnp.float32)]
    reduce_sum x5 -> x0, other arithmetic: 6.49 us -> none  [the longest x1 1.69 us: per_device(): row_total = lax.psum(jnp.sum(hidden_vals, axis=1), 'mp')]
    convert_element_type x3 -> x1, other arithmetic: 10.3 us -> 5.51 us  [per_device(): return (loss, grad_proj.astype(f32), grad_feats, sums[0], sums[1])]
  transfers between devices with their start and end apart: 4 -> 0, of which waited for: 3 -> 0; matrix products, arithmetic and copies ran while one was open for 4% -> 0% of each run, Pallas kernels for 0% -> 0%
where the time goes in v1:
time: 150 us; the launch traced here: 149 us
  Pallas kernels  136 us (91%)
  local copies, waits for them, and re-layouts  5.93 us (4%)
  other arithmetic  5.51 us (4%)
  between operations  2.43 us (2%)
    pallas_call x1, Pallas kernels, per_device(): pl.pallas_call(functools.partial(kernel, n_dp, n_mp, dt), out_shape=(jax....  136 us
    convert_element_type x1, other arithmetic, per_device(): return (loss, grad_proj.astype(f32), grad_feats, sums[0], sums[1])  5.51 us

profile of v1, /device:TPU:0, one launch (start us, length us, event | category | flops | bytes accessed | tf_op | source)
XLA Modules:
  0.0 149.4 jit_solution(11666602754472531607)
XLA Ops:
  0.6 1.3 reshape.24.tg
  1.9 1.3 reshape.25.tb
  3.2 135.6 %shard_map.110 = (bf16[1024,1536]{1,0:T(8,128)(2,1)}, bf16[128,1024]{1,0:T(8,128)(2,1)}, f32[8,1024]{1,0:T(8,128)}) custom-call(bf16[512,1536]{1,0:T(8,128)(2,1)} %th.1, f32[1,1536]{1,0:T(1,128)} %reshape.24.tg, f32[1,1536]{1,0:T(1,128)} %reshape.25.tb, bf16[128,1024]{1,0:T(8,128)(2,1)} %sf.1, f32[1,1024]{1,0:T(1,128)} %bitcast.5, f32[1,1024]{1,0:T(1,128)} %bitcast.6, ...), custom_call_target="tpu_custom_call" | custom-call | tf_op jit(solution)/shard_map/pallas_call | solution.py:433
  138.8 1.2 slice.9
  140.6 1.4 fusion
  142.1 0.0 copy-start
  142.1 5.5 %convert_element_type.3 = f32[1024,1536]{1,0:T(8,128)} convert(bf16[1024,1536]{1,0:T(8,128)(2,1)} %get-tuple-element.9) | non-fusion elementwise | flops 1572864 | bytes 9437184 | tf_op jit(solution)/shard_map/convert_element_type | solution.py:448
  147.6 0.0 copy-done
  147.6 0.7 copy.13
Async XLA Ops:
  142.1 5.5 %copy-start = (bf16[128,1024]{1,0:T(8,128)(2,1)S(1)}, bf16[128,1024]{1,0:T(8,128)(2,1)}, u32[]{:S(2)}) copy-start(bf16[128,1024]{1,0:T(8,128)(2,1)} %get-tuple-element.20) | copy-start | bytes 786436

commit v2 on v1

v2 whole, which is shorter than its diff:
```python
import functools

import jax
import jax.numpy as jnp
from jax import lax
from jax.experimental import pallas as pl
from jax.experimental.pallas import tpu as pltpu
from jax.sharding import PartitionSpec as P

epsilon = 1e-06
loss_scale = 512.0
CHUNK = 64
f32 = jnp.float32
bf16 = jnp.bfloat16


def column_tile(width, most):
    tile = most
    while width % tile:
        tile -= 128
    return tile


def split_columns(cols):
    unit = 256 if cols % 256 == 0 and cols >= 1024 else 128
    n = cols // unit
    last = max(1, (n + 3) // 6)
    first = (n - last + 1) // 2
    cuts = [0, first * unit, (n - last) * unit, cols]
    return list(zip(cuts[:-1], cuts[1:]))


def kernel(
    n_dp, n_mp, dt,
    th, tg_ref, tb_ref, sf, sg_ref, sb_ref, w,
    gp_out, gf_out, gain_out, bias_out, loss_out,
    wfull, gfull, normed, normed_t, own_hat, own_rs, target, proj, go, coef,
    stat_one, stat_two, pb, own_part, rx, zl, zr, zs, b_part, b_zl, b_zr, b_zs, b_x, gn_send, gn_recv,
    red_mp, red_x, red_z, red_a,
    ag_sems, gg_sems, nm_sems, s1_sems, s2_sems, gn_sems, rm_sems, rz_sems, rx_sems, rs_sems, rb_sems, bx_sems,
):
    length = n_dp // 2
    me = lax.axis_index("dp")
    m = lax.axis_index("mp")
    l = me // 2
    p = me % 2
    q = 1 - p
    x_dev = l * 2 + q
    right_dev = lax.rem(me + 2, n_dp)
    left_dev = lax.rem(me - 2 + n_dp, n_dp)
    tokens, cols = th.shape
    own, width = sf.shape
    rb = w.shape[0]
    chunks = split_columns(cols)
    tg, tb = tg_ref[...].reshape(1, cols), tb_ref[...].reshape(1, cols)
    sg, sb = sg_ref[...].reshape(1, width), sb_ref[...].reshape(1, width)

    def rows(j, n):
        return pl.ds(pl.multiple_of(j * n, n), n)

    def span(chunk):
        return pl.ds(chunk[0], chunk[1] - chunk[0])

    def remote(src, dst, ssem, rsem, device):
        return pltpu.make_async_remote_copy(
            src_ref=src, dst_ref=dst, send_sem=ssem, recv_sem=rsem,
            device_id=device, device_id_type=pl.DeviceIdType.MESH,
        )

    barrier = pltpu.get_barrier_semaphore()
    for k in range(1, n_mp):
        pl.semaphore_signal(barrier, inc=1, device_id={"mp": (m + k) % n_mp}, device_id_type=pl.DeviceIdType.MESH)
    for k in range(1, length):
        pl.semaphore_signal(
            barrier, inc=1, device_id={"dp": ((l + k) % length) * 2 + p}, device_id_type=pl.DeviceIdType.MESH
        )
    pl.semaphore_signal(barrier, inc=1, device_id={"dp": x_dev}, device_id_type=pl.DeviceIdType.MESH)
    pl.semaphore_wait(barrier, n_mp - 1 + length - 1 + 1)

    class Gather:
        def __init__(self, buf, sems, chunk, line_first):
            self.buf, self.sems, self.chunk, self.line_first = buf, sems, chunk, line_first
            self.lines = ((0, p),) if line_first else ((0, p), (1, q))

        def copy(self, lp, pp, ssem, rsem, device):
            ref = self.buf.at[rows(lp * 2 + pp, rb), span(self.chunk)]
            return remote(ref, ref, self.sems.at[ssem, lp], self.sems.at[rsem, lp], {"dp": device})

        def right(self, lp, pp, k):
            return self.copy(lp, pp, k, 2 + k, right_dev)

        def left(self, lp, pp, k):
            return self.copy(lp, pp, 4 + k, 2 + k, left_dev)

        def pair(self, lp, pp):
            return self.copy(lp, pp, 6, 7, x_dev)

        def forward_right(self, lp, pp, k):
            @pl.when(l + 1 < length)
            def _():
                self.right(lp, pp, k).start()

        def forward_left(self, lp, pp, k):
            @pl.when(l >= 1)
            def _():
                self.left(lp, pp, k).start()

        def begin(self):
            self.pair(l, p).start()
            self.forward_right(l, p, 0)
            self.forward_left(l, p, 0)

        def middle(self):
            self.pair(l, q).wait_recv()
            self.forward_right(l, q, 1)
            self.forward_left(l, q, 1)

        def step(self, s):
            a = l - s - 1
            b = l + s + 1
            for k, pp in self.lines:
                @pl.when(a >= 0)
                def _():
                    self.right(a, pp, k).wait_recv()
                    self.forward_right(a, pp, k)
                    if self.line_first:
                        self.pair(a, pp).start()

                @pl.when(b < length)
                def _():
                    self.left(b, pp, k).wait_recv()
                    self.forward_left(b, pp, k)
                    if self.line_first:
                        self.pair(b, pp).start()

        def finish(self):
            if self.line_first:
                @pl.loop(0, length)
                def _(lp):
                    self.pair(lp, q).wait_recv()

        def drain(self):
            @pl.loop(0, length)
            def _(lp):
                if self.line_first:
                    self.pair(lp, p).wait_send()
                for k, pp in self.lines:
                    @pl.when(jnp.logical_and(lp <= l, l + 1 < length))
                    def _():
                        self.right(lp, pp, k).wait_send()

                    @pl.when(jnp.logical_and(lp >= l, l >= 1))
                    def _():
                        self.left(lp, pp, k).wait_send()
            if not self.line_first:
                self.pair(l, p).wait_send()

    def gathers(buf, sems):
        return [Gather(buf, sems.at[i], chunks[i], i < 2) for i in range(3)]

    def mp_peers(make, act):
        for k in range(1, n_mp):
            act(make((m + k) % n_mp))

    def send_all(src, slots, sems):
        mp_peers(lambda d: remote(src(d), slots.at[m], sems.at[0, d], sems.at[1, m], {"mp": d}), lambda c: c.start())

    def recv_all(src, slots, sems):
        mp_peers(lambda d: remote(src(d), slots.at[d], sems.at[0, d], sems.at[1, d], {"mp": d}), lambda c: c.wait_recv())

    def drain_all(src, slots, sems):
        mp_peers(lambda d: remote(src(d), slots.at[m], sems.at[0, d], sems.at[1, m], {"mp": d}), lambda c: c.wait_send())

    gather_w = gathers(wfull, ag_sems)
    wfull[rows(me, rb)] = w[...]
    for g in (gather_w[2], gather_w[0], gather_w[1]):
        g.begin()

    for c in range(own // CHUNK):
        r = pl.ds(c * CHUNK, CHUNK)
        v = sf[r].astype(f32)
        v = v - jnp.mean(v, axis=1, keepdims=True)
        rs = lax.rsqrt(jnp.mean(v * v, axis=1, keepdims=True) + epsilon)
        hat = v * rs
        own_hat[r] = hat
        own_rs[r] = jnp.broadcast_to(rs, (CHUNK, 128))
        normed[m, r] = (hat * sg + sb).astype(bf16)
    nm_src = lambda d: normed.at[m]
    send_all(nm_src, normed, nm_sems)

    lane = lax.broadcasted_iota(jnp.int32, (CHUNK, 128), 1)

    @pl.loop(0, tokens // CHUNK)
    def _(c):
        r = rows(c, CHUNK)
        v = th[r].astype(f32)
        mean = jnp.sum(v, axis=1, keepdims=True) / cols
        v = v - mean
        sq = jnp.sum(v * v, axis=1, keepdims=True)
        coef[r] = jnp.where(lane == 0, mean, jnp.where(lane == 1, sq, 0.0))

    stat_one[m] = coef[...].T[0:8]
    s1_src = lambda d: stat_one.at[m]
    send_all(s1_src, stat_one, s1_sems)
    recv_all(s1_src, stat_one, s1_sems)
    mean = stat_one[0, 0:1]
    for k in range(1, n_mp):
        mean = mean + stat_one[k, 0:1]
    mean = mean / n_mp
    total = jnp.zeros_like(mean)
    for k in range(n_mp):
        gap = stat_one[k, 0:1] - mean
        total = total + (stat_one[k, 1:2] + cols * (gap * gap))
    scale = lax.rsqrt(total / dt + epsilon)
    coef[...] = jnp.concatenate([mean, scale, jnp.zeros((126, tokens), f32)], axis=0).T

    @pl.loop(0, tokens // CHUNK)
    def _(c):
        r = rows(c, CHUNK)
        cf = coef[r]
        t = (th[r].astype(f32) - cf[:, 0:1]) * cf[:, 1:2] * tg + tb
        target[r] = t
        coef[r] = jnp.where(lane == 2, jnp.sum(t * t, axis=1, keepdims=True), 0.0)

    gather_w[2].middle()
    for g in gather_w:
        g.step(0)
    recv_all(nm_src, normed, nm_sems)
    for k in range(n_mp):
        normed_t[:, pl.ds(k * own, own)] = normed[k].T

    @pl.loop(1, length - 1)
    def _(s):
        for g in gather_w:
            g.step(s)

    for g, (c0, c1) in zip(gather_w, chunks):
        g.finish()
        tile = column_tile(c1 - c0, 256)

        @pl.loop(0, (c1 - c0) // tile)
        def _(c):
            ct = pl.ds(pl.multiple_of(c0 + c * tile, 128), tile)
            proj[:, ct] = jnp.dot(
                normed[...].reshape(tokens, width), wfull[:, ct], preferred_element_type=f32
            )

        @pl.loop(0, tokens // CHUNK)
        def _(c):
            r = rows(c, CHUNK)
            pv, t = proj[r, c0:c1], target[r, c0:c1]
            inner = jnp.sum(pv * t, axis=1, keepdims=True)
            sq = jnp.sum(pv * pv, axis=1, keepdims=True)
            coef[r] = coef[r] + jnp.where(lane == 0, inner, jnp.where(lane == 1, sq, 0.0))

    stat_two[m] = coef[...].T[0:8]
    s2_src = lambda d: stat_two.at[m]
    send_all(s2_src, stat_two, s2_sems)
    recv_all(s2_src, stat_two, s2_sems)
    sums = stat_two[0]
    for k in range(1, n_mp):
        sums = sums + stat_two[k]
    inner = sums[0:1]
    norm_proj = jnp.sqrt(sums[1:2] + epsilon)
    norm_target = jnp.sqrt(sums[2:3] + epsilon)
    both = norm_proj * norm_target
    loss_part = jnp.sum(1.0 - inner / both, axis=1, keepdims=True)
    coef_proj = loss_scale * inner / (norm_proj * norm_proj * norm_proj * norm_target)
    coef_target = loss_scale / both
    coef[...] = jnp.concatenate([coef_proj, coef_target, jnp.zeros((126, tokens), f32)], axis=0).T

    def make_go(chunk):
        @pl.loop(0, tokens // CHUNK)
        def _(c):
            r = rows(c, CHUNK)
            cf = coef[r]
            ct = span(chunk)
            go[r, ct] = (cf[:, 0:1] * proj[r, ct] - cf[:, 1:2] * target[r, ct]).astype(bf16)

    near = jnp.minimum(l, length - 1 - l)
    alone = length - 1 - 2 * near

    def order(i):
        far = jnp.where(2 * l < length, length - 1 - i, i)
        k = jnp.maximum(i - alone, 0)
        d = near - k // 2
        return jnp.where(i < alone, far, jnp.where(k % 2 == 0, l + d, l - d))

    def partial(j, chunk):
        return jnp.dot(normed_t[rows(j, rb)], go[:, span(chunk)], preferred_element_type=f32)

    def x_copy(i, lp):
        part = span(chunks[i])
        return remote(pb.at[lp, :, part], rx.at[lp, :, part], rs_sems.at[i, 0, lp], rs_sems.at[i, 1, lp], {"dp": x_dev})

    def right_copy(i, lp):
        part = span(chunks[i])
        return remote(
            zs.at[lp, :, part], zl.at[lp, :, part], rs_sems.at[i, 2, lp], rs_sems.at[i, 3, lp], {"dp": right_dev}
        )

    def left_copy(i, lp):
        part = span(chunks[i])
        return remote(
            zs.at[lp, :, part], zr.at[lp, :, part], rs_sems.at[i, 4, lp], rs_sems.at[i, 5, lp], {"dp": left_dev}
        )

    def b_right(lp):
        return remote(b_zs.at[lp], b_zl.at[lp], rb_sems.at[0, lp], rb_sems.at[1, lp], {"dp": right_dev})

    def b_left(lp):
        return remote(b_zs.at[lp], b_zr.at[lp], rb_sems.at[2, lp], rb_sems.at[3, lp], {"dp": left_dev})

    def b_pair():
        return remote(b_zs.at[l, q], b_x, bx_sems.at[0], bx_sems.at[1], {"dp": x_dev})

    def scatter(i, lp):
        part = span(chunks[i])
        x_copy(i, lp).wait_recv()

        @pl.when(jnp.logical_and(lp >= l, l > 0))
        def _():
            right_copy(i, lp).wait_recv()
            own_part[lp, :, part] = own_part[lp, :, part] + zl[lp, :, part].astype(f32)

        @pl.when(jnp.logical_and(lp <= l, l < length - 1))
        def _():
            left_copy(i, lp).wait_recv()
            own_part[lp, :, part] = own_part[lp, :, part] + zr[lp, :, part].astype(f32)

        zs[lp, :, part] = (own_part[lp, :, part] + rx[lp, :, part].astype(f32)).astype(bf16)

        @pl.when(lp > l)
        def _():
            right_copy(i, lp).start()

        @pl.when(lp < l)
        def _():
            left_copy(i, lp).start()

    def b_scatter(lp):
        @pl.when(jnp.logical_and(lp >= l, l > 0))
        def _():
            b_right(lp).wait_recv()
            b_part[lp] = b_part[lp] + b_zl[lp].astype(f32)

        @pl.when(jnp.logical_and(lp <= l, l < length - 1))
        def _():
            b_left(lp).wait_recv()
            b_part[lp] = b_part[lp] + b_zr[lp].astype(f32)

        b_zs[lp] = b_part[lp].astype(bf16)

        @pl.when(lp > l)
        def _():
            b_right(lp).start()

        @pl.when(lp < l)
        def _():
            b_left(lp).start()

        @pl.when(lp == l)
        def _():
            b_pair().start()

    last = chunks[2]
    make_go(last)
    b_part[...] = jnp.dot(normed_t[...], go[:, span(last)], preferred_element_type=f32).reshape(b_part.shape)

    at_end = jnp.logical_or(l == 0, l == length - 1)

    @pl.when(at_end)
    def _():
        @pl.loop(0, length - 1)
        def _(n):
            b_scatter(order(n))

    for i in range(2):
        make_go(chunks[i])

        @pl.loop(0, length)
        def _(n):
            lp = order(n)
            pb[lp, :, span(chunks[i])] = partial(lp * 2 + q, chunks[i]).astype(bf16)
            x_copy(i, lp).start()

    for i in range(2):
        @pl.loop(0, length)
        def _(n):
            lp = order(n)
            own_part[lp, :, span(chunks[i])] = partial(lp * 2 + p, chunks[i])

    band = 256

    @pl.loop(0, width // band)
    def _(c):
        ct = rows(c, band)
        g = lax.dot_general(go[...], wfull[ct], (((1,), (1,)), ((), ())), preferred_element_type=f32)
        for k in range(n_mp):
            gn_send[k, :, ct] = g[k * own:(k + 1) * own].astype(bf16)

    gn_src = lambda d: gn_send.at[d]
    send_all(gn_src, gn_recv, gn_sems)
    gn_recv[m] = gn_send[m]

    gather_g = gathers(gfull, gg_sems)

    @pl.loop(0, length)
    def _(n):
        lp = order(n)

        @pl.when(jnp.logical_or(jnp.logical_not(at_end), n == length - 1))
        def _():
            b_scatter(lp)

        scatter(0, lp)

    gfull[rows(me, rb), span(chunks[0])] = zs[l, :, span(chunks[0])]
    gather_g[0].begin()

    scatter(1, order(0))
    b_pair().wait_recv()
    gfull[rows(me, rb), span(last)] = (b_part[l, p] + b_x[...].astype(f32)).astype(bf16)
    gather_g[2].begin()

    recv_all(gn_src, gn_recv, gn_sems)
    gain_sum = jnp.zeros((1, width), f32)
    bias_sum = jnp.zeros((1, width), f32)
    for c in range(own // CHUNK):
        r = pl.ds(c * CHUNK, CHUNK)
        g = gn_recv[0, r].astype(f32)
        for k in range(1, n_mp):
            g = g + gn_recv[k, r].astype(f32)
        hat = own_hat[r]
        gain_sum = gain_sum + jnp.sum(g * hat, axis=0, keepdims=True)
        bias_sum = bias_sum + jnp.sum(g, axis=0, keepdims=True)
        g = g * sg
        g = g - jnp.mean(g, axis=1, keepdims=True) - hat * jnp.mean(g * hat, axis=1, keepdims=True)
        gf_out[r] = (own_rs[r][:, 0:1] * g).astype(bf16)
    red_mp[m] = jnp.concatenate(
        [gain_sum, bias_sum, jnp.broadcast_to(loss_part, (1, width)), jnp.zeros((5, width), f32)], axis=0
    )
    rm_src = lambda d: red_mp.at[m]
    send_all(rm_src, red_mp, rm_sems)
    gather_g[0].step(0)
    gather_g[2].middle()

    @pl.loop(1, length - 1)
    def _(n):
        scatter(1, order(n))
        gather_g[0].step(n)
        gather_g[2].step(n - 1)

    scatter(1, order(length - 1))
    gfull[rows(me, rb), span(chunks[1])] = zs[l, :, span(chunks[1])]
    gather_g[1].begin()
    gather_g[2].step(length - 2)

    recv_all(rm_src, red_mp, rm_sems)
    acc = red_mp[0]
    for k in range(1, n_mp):
        acc = acc + red_mp[k]
    red_a[...] = acc
    pair = remote(red_a, red_x, rx_sems.at[0], rx_sems.at[1], {"dp": x_dev})
    pair.start()
    gather_g[1].step(0)
    pair.wait_recv()
    red_z[l] = red_a[...] + red_x[...]

    def line_copy(d, slot):
        return remote(red_z.at[l], red_z.at[slot], rz_sems.at[0, d], rz_sems.at[1, slot], {"dp": d * 2 + p})

    for k in range(1, length):
        line_copy((l + k) % length, l).start()

    @pl.loop(1, length - 1)
    def _(s):
        gather_g[1].step(s)

    for k in range(1, length):
        line_copy((l + k) % length, (l + k) % length).wait_recv()
    acc = red_z[0]
    for k in range(1, length):
        acc = acc + red_z[k]
    gain_out[...] = acc[0:1].reshape(width)
    bias_out[...] = acc[1:2].reshape(width)
    loss_out[...] = acc[2:3, 0:128] / (n_mp * tokens * n_dp)

    gather_g[0].finish()
    gather_g[2].finish()
    gather_g[1].finish()
    gp_out[...] = gfull[...]

    for g in gather_w + gather_g:
        g.drain()
    drain_all(nm_src, normed, nm_sems)
    drain_all(s1_src, stat_one, s1_sems)
    drain_all(s2_src, stat_two, s2_sems)
    drain_all(gn_src, gn_recv, gn_sems)
    drain_all(rm_src, red_mp, rm_sems)
    pair.wait_send()
    for k in range(1, length):
        line_copy((l + k) % length, l).wait_send()
    b_pair().wait_send()

    @pl.loop(0, length)
    def _(lp):
        for i in range(2):
            x_copy(i, lp).wait_send()

        @pl.when(lp > l)
        def _():
            for i in range(2):
                right_copy(i, lp).wait_send()
            b_right(lp).wait_send()

        @pl.when(lp < l)
        def _():
            for i in range(2):
                left_copy(i, lp).wait_send()
            b_left(lp).wait_send()


def per_device(n_dp, n_mp, dt, th, tg, tb, sf, sg, sb, w):
    tokens, cols = th.shape
    own, width = sf.shape
    rb = w.shape[0]
    length = n_dp // 2
    chunks = split_columns(cols)
    bw = chunks[2][1] - chunks[2][0]
    vmem = pltpu.VMEM
    dma = pltpu.SemaphoreType.DMA
    scratch = [
        vmem((width, cols), bf16),
        vmem((width, cols), bf16),
        vmem((n_mp, own, width), bf16),
        vmem((width, tokens), bf16),
        vmem((own, width), f32),
        vmem((own, 128), f32),
        vmem((tokens, cols), f32),
        vmem((tokens, cols), f32),
        vmem((tokens, cols), bf16),
        vmem((tokens, 128), f32),
        vmem((n_mp, 8, tokens), f32),
        vmem((n_mp, 8, tokens), f32),
        vmem((length, rb, cols), bf16),
        vmem((length, rb, cols), f32),
        vmem((length, rb, cols), bf16),
        vmem((length, rb, cols), bf16),
        vmem((length, rb, cols), bf16),
        vmem((length, rb, cols), bf16),
        vmem((length, 2, rb, bw), f32),
        vmem((length, 2, rb, bw), bf16),
        vmem((length, 2, rb, bw), bf16),
        vmem((length, 2, rb, bw), bf16),
        vmem((rb, bw), bf16),
        vmem((n_mp, own, width), bf16),
        vmem((n_mp, own, width), bf16),
        vmem((n_mp, 8, width), f32),
        vmem((8, width), f32),
        vmem((length, 8, width), f32),
        vmem((8, width), f32),
        dma((3, 8, length)), dma((3, 8, length)),
        dma((2, n_mp)), dma((2, n_mp)), dma((2, n_mp)), dma((2, n_mp)), dma((2, n_mp)),
        dma((2, length)), dma((2,)), dma((2, 6, length)), dma((4, length)), dma((2,)),
    ]
    whole = pl.BlockSpec(memory_space=pltpu.VMEM)
    grad_proj, grad_feats, gain, bias, loss = pl.pallas_call(
        functools.partial(kernel, n_dp, n_mp, dt),
        out_shape=(
            jax.ShapeDtypeStruct((width, cols), bf16),
            jax.ShapeDtypeStruct((own, width), bf16),
            jax.ShapeDtypeStruct((width,), f32),
            jax.ShapeDtypeStruct((width,), f32),
            jax.ShapeDtypeStruct((1, 128), f32),
        ),
        in_specs=[whole] * 7,
        out_specs=(whole,) * 5,
        scratch_shapes=scratch,
        compiler_params=pltpu.CompilerParams(
            collective_id=0, has_side_effects=True, vmem_limit_bytes=56 * 1024 * 1024
        ),
    )(th, tg, tb, sf, sg, sb, w)
    return (loss[0, 0], grad_proj.astype(f32), grad_feats, gain, bias)


def solution(mesh):
    n_dp, n_mp = mesh.shape["dp"], mesh.shape["mp"]

    def run(th, tg, tb, sf, sg, sb, w):
        in_specs = (P("dp", "mp"), P("mp"), P("mp"), P(("dp", "mp"), None), P(), P(), P("dp", "mp"))
        out_specs = (P(), P(None, "mp"), P(("dp", "mp"), None), P(), P())
        return jax.shard_map(
            functools.partial(per_device, n_dp, n_mp, th.shape[1]),
            mesh=mesh, in_specs=in_specs, out_specs=out_specs, check_vma=False,
        )(th, tg, tb, sf, sg, sb, w)

    return run
```

time: 150 us -> 143 us (0.953)
  local copies, waits for them, and re-layouts: 5.93 us -> 1.91 us
  Pallas kernels: 136 us -> 134 us
    slice x2 -> x0, local copies, waits for them, and re-layouts: 2.63 us -> none  [the longest x1 1.44 us: per_device(): return (loss, grad_proj.astype(f32), grad_feats, sums[0], sums[1])]
    reshape x2 -> x0, local copies, waits for them, and re-layouts: 2.59 us -> none  [the longest x1 1.3 us: per_device(): tg.reshape(1, -1)]
    pallas_call x1, Pallas kernels: 136 us -> 134 us  [per_device(): pl.pallas_call(functools.partial(kernel, n_dp, n_mp, dt), out_shape=(jax....]
where the time goes in v2:
time: 143 us
  Pallas kernels  134 us (94%)
  other arithmetic  5.5 us (4%)
  local copies, waits for them, and re-layouts  1.91 us (1%)
  between operations  1.85 us (1%)
    pallas_call x1, Pallas kernels, per_device(): pl.pallas_call(functools.partial(kernel, n_dp, n_mp, dt), out_shape=(jax....  134 us
    convert_element_type x1, other arithmetic, per_device(): return (loss[0, 0], grad_proj.astype(f32), grad_feats, gain, bias)  5.5 us

profile of v2, /device:TPU:0, one launch (start us, length us, event | category | flops | bytes accessed | tf_op | source)
XLA Modules:
  0.0 142.8 jit_solution(4512807766499675808)
XLA Ops:
  0.6 133.5 %shard_map.110 = (bf16[1024,1536]{1,0:T(8,128)(2,1)}, bf16[128,1024]{1,0:T(8,128)(2,1)}, f32[1024]{0:T(1024)}, f32[1024]{0:T(1024)}, f32[1,128]{1,0:T(1,128)}) custom-call(bf16[512,1536]{1,0:T(8,128)(2,1)} %th.1, f32[1536]{0:T(1024)} %tg_ref.1, f32[1536]{0:T(1024)} %tb_ref.1, bf16[128,1024]{1,0:T(8,128)(2,1)} %sf.1, f32[1024]{0:T(1024)} %sg_ref.1, ...), custom_call_target="tpu_custom_call" | custom-call | tf_op jit(solution)/shard_map/pallas_call | solution.py:568
  134.1 0.0 copy-start.3
  134.2 0.0 copy-start
  134.2 0.0 copy-start.2
  134.2 0.0 copy-start.1
  134.2 5.5 %convert_element_type.3 = f32[1024,1536]{1,0:T(8,128)} convert(bf16[1024,1536]{1,0:T(8,128)(2,1)} %get-tuple-element.11) | non-fusion elementwise | flops 1572864 | bytes 9437184 | tf_op jit(solution)/shard_map/convert_element_type | solution.py:584
  139.7 0.0 copy-done.3
  139.7 0.0 copy-done
  139.7 0.7 copy.17
  140.4 0.0 copy-done.2
  140.4 0.6 copy.18
  141.0 0.0 copy-done.1
  141.0 0.6 copy.19
Async XLA Ops:
  134.1 5.5 %copy-start.3 = (f32[1,128]{1,0:T(1,128)S(1)}, f32[1,128]{1,0:T(1,128)}, u32[]{:S(2)}) copy-start(f32[1,128]{1,0:T(1,128)} %get-tuple-element.10) | copy-start | bytes 1540
  134.2 5.6 %copy-start = (bf16[128,1024]{1,0:T(8,128)(2,1)S(1)}, bf16[128,1024]{1,0:T(8,128)(2,1)}, u32[]{:S(2)}) copy-start(bf16[128,1024]{1,0:T(8,128)(2,1)} %get-tuple-element.22) | copy-start | bytes 786436
  134.2 6.3 %copy-start.2 = (f32[1024]{0:T(1024)S(1)}, f32[1024]{0:T(1024)}, u32[]{:S(2)}) copy-start(f32[1024]{0:T(1024)} %get-tuple-element.23) | copy-start | bytes 12292
  134.2 6.9 %copy-start.1 = (f32[1024]{0:T(1024)S(1)}, f32[1024]{0:T(1024)}, u32[]{:S(2)}) copy-start(f32[1024]{0:T(1024)} %get-tuple-element.24) | copy-start | bytes 12292

commit v3 on v2

--- a/solution.py
+++ b/solution.py
@@ -10,6 +10,7 @@
 epsilon = 1e-06
 loss_scale = 512.0
 CHUNK = 64
+WINDOW = 4
 f32 = jnp.float32
 bf16 = jnp.bfloat16
 
@@ -176,6 +177,20 @@
     for g in (gather_w[2], gather_w[0], gather_w[1]):
         g.begin()
 
+    lane = lax.broadcasted_iota(jnp.int32, (CHUNK, 128), 1)
+
+    @pl.loop(0, tokens // CHUNK)
+    def _(c):
+        r = rows(c, CHUNK)
+        v = th[r].astype(f32)
+        mean = jnp.sum(v, axis=1, keepdims=True) / cols
+        v = v - mean
+        sq = jnp.sum(v * v, axis=1, keepdims=True)
+        coef[r] = jnp.where(lane == 0, mean, jnp.where(lane == 1, sq, 0.0))
+
+    stat_one[m] = coef[...].T[0:8]
+    s1_src = lambda d: stat_one.at[m]
+    send_all(s1_src, stat_one, s1_sems)
     for c in range(own // CHUNK):
         r = pl.ds(c * CHUNK, CHUNK)
         v = sf[r].astype(f32)
@@ -188,20 +203,9 @@
     nm_src = lambda d: normed.at[m]
     send_all(nm_src, normed, nm_sems)
 
-    lane = lax.broadcasted_iota(jnp.int32, (CHUNK, 128), 1)
-
-    @pl.loop(0, tokens // CHUNK)
-    def _(c):
-        r = rows(c, CHUNK)
-        v = th[r].astype(f32)
-        mean = jnp.sum(v, axis=1, keepdims=True) / cols
-        v = v - mean
-        sq = jnp.sum(v * v, axis=1, keepdims=True)
-        coef[r] = jnp.where(lane == 0, mean, jnp.where(lane == 1, sq, 0.0))
-
-    stat_one[m] = coef[...].T[0:8]
-    s1_src = lambda d: stat_one.at[m]
-    send_all(s1_src, stat_one, s1_sems)
+    gather_w[2].middle()
+    for g in gather_w:
+        g.step(0)
     recv_all(s1_src, stat_one, s1_sems)
     mean = stat_one[0, 0:1]
     for k in range(1, n_mp):
@@ -222,9 +226,6 @@
         target[r] = t
         coef[r] = jnp.where(lane == 2, jnp.sum(t * t, axis=1, keepdims=True), 0.0)
 
-    gather_w[2].middle()
-    for g in gather_w:
-        g.step(0)
     recv_all(nm_src, normed, nm_sems)
     for k in range(n_mp):
         normed_t[:, pl.ds(k * own, own)] = normed[k].T
@@ -314,9 +315,11 @@
     def b_pair():
         return remote(b_zs.at[l, q], b_x, bx_sems.at[0], bx_sems.at[1], {"dp": x_dev})
 
-    def scatter(i, lp):
+    def scatter(i, n):
+        lp = order(n)
         part = span(chunks[i])
         x_copy(i, lp).wait_recv()
+        x_start(i * length + n + WINDOW)
 
         @pl.when(jnp.logical_and(lp >= l, l > 0))
         def _():
@@ -363,10 +366,31 @@
         def _():
             b_pair().start()
 
+    def x_start(k):
+        @pl.when(k < length)
+        def _():
+            x_copy(0, order(k)).start()
+
+        @pl.when(jnp.logical_and(k >= length, k < 2 * length))
+        def _():
+            x_copy(1, order(k - length)).start()
+
+    def x_blocks(i):
+        make_go(chunks[i])
+
+        @pl.loop(0, length)
+        def _(n):
+            lp = order(n)
+            pb[lp, :, span(chunks[i])] = partial(lp * 2 + q, chunks[i]).astype(bf16)
+            if i == 0:
+                @pl.when(n < WINDOW)
+                def _():
+                    x_start(n)
+
+    x_blocks(0)
     last = chunks[2]
     make_go(last)
     b_part[...] = jnp.dot(normed_t[...], go[:, span(last)], preferred_element_type=f32).reshape(b_part.shape)
-
     at_end = jnp.logical_or(l == 0, l == length - 1)
 
     @pl.when(at_end)
@@ -375,14 +399,7 @@
         def _(n):
             b_scatter(order(n))
 
-    for i in range(2):
-        make_go(chunks[i])
-
-        @pl.loop(0, length)
-        def _(n):
-            lp = order(n)
-            pb[lp, :, span(chunks[i])] = partial(lp * 2 + q, chunks[i]).astype(bf16)
-            x_copy(i, lp).start()
+    x_blocks(1)
 
     for i in range(2):
         @pl.loop(0, length)
@@ -413,12 +430,12 @@
         def _():
             b_scatter(lp)
 
-        scatter(0, lp)
+        scatter(0, n)
 
     gfull[rows(me, rb), span(chunks[0])] = zs[l, :, span(chunks[0])]
     gather_g[0].begin()
 
-    scatter(1, order(0))
+    scatter(1, 0)
     b_pair().wait_recv()
     gfull[rows(me, rb), span(last)] = (b_part[l, p] + b_x[...].astype(f32)).astype(bf16)
     gather_g[2].begin()
@@ -447,11 +464,11 @@
 
     @pl.loop(1, length - 1)
     def _(n):
-        scatter(1, order(n))
+        scatter(1, n)
         gather_g[0].step(n)
         gather_g[2].step(n - 1)
 
-    scatter(1, order(length - 1))
+    scatter(1, length - 1)
     gfull[rows(me, rb), span(chunks[1])] = zs[l, :, span(chunks[1])]
     gather_g[1].begin()
     gather_g[2].step(length - 2)

time: 143 us -> 136 us (0.951)
  Pallas kernels: 134 us -> 126 us
    pallas_call x1, Pallas kernels: 134 us -> 126 us  [per_device(): pl.pallas_call(functools.partial(kernel, n_dp, n_mp, dt), out_shape=(jax....]
where the time goes in v3:
time: 136 us
  Pallas kernels  126 us (93%)
  other arithmetic  5.5 us (4%)
  local copies, waits for them, and re-layouts  1.91 us (1%)
  between operations  1.85 us (1%)
    pallas_call x1, Pallas kernels, per_device(): pl.pallas_call(functools.partial(kernel, n_dp, n_mp, dt), out_shape=(jax....  126 us
    convert_element_type x1, other arithmetic, per_device(): return (loss[0, 0], grad_proj.astype(f32), grad_feats, gain, bias)  5.5 us

profile of v3, /device:TPU:0, one launch (start us, length us, event | category | flops | bytes accessed | tf_op | source)
XLA Modules:
  0.0 135.5 jit_solution(14305121495552463273)
XLA Ops:
  0.6 126.3 %shard_map.110 = (bf16[1024,1536]{1,0:T(8,128)(2,1)}, bf16[128,1024]{1,0:T(8,128)(2,1)}, f32[1024]{0:T(1024)}, f32[1024]{0:T(1024)}, f32[1,128]{1,0:T(1,128)}) custom-call(bf16[512,1536]{1,0:T(8,128)(2,1)} %th.1, f32[1536]{0:T(1024)} %tg_ref.1, f32[1536]{0:T(1024)} %tb_ref.1, bf16[128,1024]{1,0:T(8,128)(2,1)} %sf.1, f32[1024]{0:T(1024)} %sg_ref.1, ...), custom_call_target="tpu_custom_call" | custom-call | tf_op jit(solution)/shard_map/pallas_call | solution.py:585
  126.9 0.0 copy-start.3
  126.9 0.0 copy-start
  126.9 0.0 copy-start.2
  127.0 0.0 copy-start.1
  127.0 5.5 %convert_element_type.3 = f32[1024,1536]{1,0:T(8,128)} convert(bf16[1024,1536]{1,0:T(8,128)(2,1)} %get-tuple-element.11) | non-fusion elementwise | flops 1572864 | bytes 9437184 | tf_op jit(solution)/shard_map/convert_element_type | solution.py:601
  132.5 0.0 copy-done.3
  132.5 0.0 copy-done
  132.5 0.7 copy.17
  133.2 0.0 copy-done.2
  133.2 0.6 copy.18
  133.8 0.0 copy-done.1
  133.8 0.6 copy.19
Async XLA Ops:
  126.9 5.5 %copy-start.3 = (f32[1,128]{1,0:T(1,128)S(1)}, f32[1,128]{1,0:T(1,128)}, u32[]{:S(2)}) copy-start(f32[1,128]{1,0:T(1,128)} %get-tuple-element.10) | copy-start | bytes 1540
  126.9 5.6 %copy-start = (bf16[128,1024]{1,0:T(8,128)(2,1)S(1)}, bf16[128,1024]{1,0:T(8,128)(2,1)}, u32[]{:S(2)}) copy-start(bf16[128,1024]{1,0:T(8,128)(2,1)} %get-tuple-element.22) | copy-start | bytes 786436
  126.9 6.3 %copy-start.2 = (f32[1024]{0:T(1024)S(1)}, f32[1024]{0:T(1024)}, u32[]{:S(2)}) copy-start(f32[1024]{0:T(1024)} %get-tuple-element.23) | copy-start | bytes 12292
  127.0 6.9 %copy-start.1 = (f32[1024]{0:T(1024)S(1)}, f32[1024]{0:T(1024)}, u32[]{:S(2)}) copy-start(f32[1024]{0:T(1024)} %get-tuple-element.24) | copy-start | bytes 12292

commit v4 on v3

--- a/solution.py
+++ b/solution.py
@@ -9,7 +9,7 @@
 
 epsilon = 1e-06
 loss_scale = 512.0
-CHUNK = 64
+CHUNK = 128
 WINDOW = 4
 f32 = jnp.float32
 bf16 = jnp.bfloat16
@@ -33,13 +33,17 @@
 
 def kernel(
     n_dp, n_mp, dt,
-    th, tg_ref, tb_ref, sf, sg_ref, sb_ref, w,
+    th_hbm, tg_ref, tb_ref, sf_hbm, sg_ref, sb_ref, w,
     gp_out, gf_out, gain_out, bias_out, loss_out,
     wfull, gfull, normed, normed_t, own_hat, own_rs, target, proj, go, coef,
     stat_one, stat_two, pb, own_part, rx, zl, zr, zs, b_part, b_zl, b_zr, b_zs, b_x, gn_send, gn_recv,
-    red_mp, red_x, red_z, red_a,
+    red_mp, red_x, red_z, red_a, th, sf, in_sems, out_sems,
     ag_sems, gg_sems, nm_sems, s1_sems, s2_sems, gn_sems, rm_sems, rz_sems, rx_sems, rs_sems, rb_sems, bx_sems,
 ):
+    load_th = pltpu.make_async_copy(th_hbm, th, in_sems.at[0])
+    load_sf = pltpu.make_async_copy(sf_hbm, sf, in_sems.at[1])
+    load_th.start()
+    load_sf.start()
     length = n_dp // 2
     me = lax.axis_index("dp")
     m = lax.axis_index("mp")
@@ -179,6 +183,9 @@
 
     lane = lax.broadcasted_iota(jnp.int32, (CHUNK, 128), 1)
 
+    load_th.wait()
+    load_sf.wait()
+
     @pl.loop(0, tokens // CHUNK)
     def _(c):
         r = rows(c, CHUNK)
@@ -399,13 +406,15 @@
         def _(n):
             b_scatter(order(n))
 
-    x_blocks(1)
-
-    for i in range(2):
-        @pl.loop(0, length)
-        def _(n):
-            lp = order(n)
-            own_part[lp, :, span(chunks[i])] = partial(lp * 2 + p, chunks[i])
+    make_go(chunks[1])
+
+    def own_block(i, n):
+        lp = order(n)
+        own_part[lp, :, span(chunks[i])] = partial(lp * 2 + p, chunks[i])
+
+    @pl.loop(0, length)
+    def _(n):
+        own_block(0, n)
 
     band = 256
 
@@ -430,7 +439,9 @@
         def _():
             b_scatter(lp)
 
+        pb[order(n), :, span(chunks[1])] = partial(order(n) * 2 + q, chunks[1]).astype(bf16)
         scatter(0, n)
+        own_block(1, n)
 
     gfull[rows(me, rb), span(chunks[0])] = zs[l, :, span(chunks[0])]
     gather_g[0].begin()
@@ -503,10 +514,13 @@
     bias_out[...] = acc[1:2].reshape(width)
     loss_out[...] = acc[2:3, 0:128] / (n_mp * tokens * n_dp)
 
-    gather_g[0].finish()
-    gather_g[2].finish()
-    gather_g[1].finish()
-    gp_out[...] = gfull[...]
+    def out_copy(i):
+        part = span(chunks[i])
+        return pltpu.make_async_copy(gfull.at[:, part], gp_out.at[:, part], out_sems.at[i])
+
+    for i in (0, 2, 1):
+        gather_g[i].finish()
+        out_copy(i).start()
 
     for g in gather_w + gather_g:
         g.drain()
@@ -519,6 +533,8 @@
     for k in range(1, length):
         line_copy((l + k) % length, l).wait_send()
     b_pair().wait_send()
+    for i in range(3):
+        out_copy(i).wait()
 
     @pl.loop(0, length)
     def _(lp):
@@ -577,11 +593,16 @@
         vmem((8, width), f32),
         vmem((length, 8, width), f32),
         vmem((8, width), f32),
+        vmem((tokens, cols), bf16),
+        vmem((own, width), bf16),
+        dma((2,)),
+        dma((3,)),
         dma((3, 8, length)), dma((3, 8, length)),
         dma((2, n_mp)), dma((2, n_mp)), dma((2, n_mp)), dma((2, n_mp)), dma((2, n_mp)),
         dma((2, length)), dma((2,)), dma((2, 6, length)), dma((4, length)), dma((2,)),
     ]
     whole = pl.BlockSpec(memory_space=pltpu.VMEM)
+    hbm = pl.BlockSpec(memory_space=pl.ANY)
     grad_proj, grad_feats, gain, bias, loss = pl.pallas_call(
         functools.partial(kernel, n_dp, n_mp, dt),
         out_shape=(
@@ -591,8 +612,8 @@
             jax.ShapeDtypeStruct((width,), f32),
             jax.ShapeDtypeStruct((1, 128), f32),
         ),
-        in_specs=[whole] * 7,
-        out_specs=(whole,) * 5,
+        in_specs=[hbm, whole, whole, hbm, whole, whole, whole],
+        out_specs=(hbm,) + (whole,) * 4,
         scratch_shapes=scratch,
         compiler_params=pltpu.CompilerParams(
             collective_id=0, has_side_effects=True, vmem_limit_bytes=56 * 1024 * 1024

time: 136 us -> 133 us (0.978)
  Pallas kernels: 126 us -> 124 us
    pallas_call x1, Pallas kernels: 126 us -> 124 us  [per_device(): pl.pallas_call(functools.partial(kernel, n_dp, n_mp, dt), out_shape=(jax....]
where the time goes in v4:
time: 133 us
  Pallas kernels  124 us (93%)
  other arithmetic  5.5 us (4%)
  local copies, waits for them, and re-layouts  1.91 us (1%)
  between operations  1.85 us (1%)
    pallas_call x1, Pallas kernels, per_device(): pl.pallas_call(functools.partial(kernel, n_dp, n_mp, dt), out_shape=(jax....  124 us
    convert_element_type x1, other arithmetic, per_device(): return (loss[0, 0], grad_proj.astype(f32), grad_feats, gain, bias)  5.5 us

profile of v4, /device:TPU:0, one launch (start us, length us, event | category | flops | bytes accessed | tf_op | source)
XLA Modules:
  0.0 133.3 jit_solution(12005886700623027236)
XLA Ops:
  0.6 124.0 %shard_map.110 = (bf16[1024,1536]{1,0:T(8,128)(2,1)}, bf16[128,1024]{1,0:T(8,128)(2,1)}, f32[1024]{0:T(1024)}, f32[1024]{0:T(1024)}, f32[1,128]{1,0:T(1,128)}) custom-call(bf16[512,1536]{1,0:T(8,128)(2,1)} %th_hbm.1, f32[1536]{0:T(1024)} %tg_ref.1, f32[1536]{0:T(1024)} %tb_ref.1, bf16[128,1024]{1,0:T(8,128)(2,1)} %sf_hbm.1, f32[1024]{0:T(1024)} %sg_ref.1, ...), custom_call_target="tpu_custom_call" | custom-call | tf_op jit(solution)/shard_map/pallas_call | solution.py:606
  124.6 0.0 copy-start.3
  124.7 0.0 copy-start
  124.7 0.0 copy-start.2
  124.7 0.0 copy-start.1
  124.7 5.5 %convert_element_type.3 = f32[1024,1536]{1,0:T(8,128)} convert(bf16[1024,1536]{1,0:T(8,128)(2,1)} %get-tuple-element.11) | non-fusion elementwise | flops 1572864 | bytes 9437184 | tf_op jit(solution)/shard_map/convert_element_type | solution.py:622
  130.2 0.0 copy-done.3
  130.2 0.0 copy-done
  130.2 0.7 copy.17
  130.9 0.0 copy-done.2
  131.0 0.6 copy.18
  131.5 0.0 copy-done.1
  131.5 0.6 copy.19
Async XLA Ops:
  124.6 5.5 %copy-start.3 = (f32[1,128]{1,0:T(1,128)S(1)}, f32[1,128]{1,0:T(1,128)}, u32[]{:S(2)}) copy-start(f32[1,128]{1,0:T(1,128)} %get-tuple-element.10) | copy-start | bytes 1540
  124.7 5.6 %copy-start = (bf16[128,1024]{1,0:T(8,128)(2,1)S(1)}, bf16[128,1024]{1,0:T(8,128)(2,1)}, u32[]{:S(2)}) copy-start(bf16[128,1024]{1,0:T(8,128)(2,1)} %get-tuple-element.22) | copy-start | bytes 786436
  124.7 6.3 %copy-start.2 = (f32[1024]{0:T(1024)S(1)}, f32[1024]{0:T(1024)}, u32[]{:S(2)}) copy-start(f32[1024]{0:T(1024)} %get-tuple-element.23) | copy-start | bytes 12292
  124.7 6.9 %copy-start.1 = (f32[1024]{0:T(1024)S(1)}, f32[1024]{0:T(1024)}, u32[]{:S(2)}) copy-start(f32[1024]{0:T(1024)} %get-tuple-element.24) | copy-start | bytes 12292
